TPU v7x, 128 devices: a whole 4x4x4 slice. The times are simulated.
128 devices in a mesh: row: 8 (over x, core), col: 16 (over z, y).
Axes of the slice: x: 4, y: 4, z: 4, core: 2. Of those that a mesh axis runs over, the one named last changes fastest.
Arguments:
- right_side: float32 [2048, 288], P(('row', 'col'))
- diag_blocks: float32 [2048, 288, 288], P(('row', 'col')), as said below
- precond: float32 [2048, 288, 288], P(('row', 'col'))
- tile_values: float32 [8, 16, 32, 288, 288], P('row', 'col'), may hold values from -0.09375 to 0.09375
- pair_rows: int32 [8, 16, 32], P('row', 'col'), may hold values from 0 to 255
- pair_cols: int32 [8, 16, 32], P('row', 'col'), may hold values from 0 to 127
- tile_counts: int32 [8, 16], P('row', 'col'), may hold values from 8 to 32, as said below
Outputs:
- solution: float32 [2048, 288], P(('row', 'col'))
- residual: float32 [2048, 288], P(('row', 'col'))
Inputs may be any that keep to these rules, and one draw needn't show every extreme that they name: `tile_counts`: slots at or beyond an owner's count hold indices that must be ignored; some owner holds exactly 32 live slots. `diag_blocks`: every diagonal block and every preconditioner block is symmetric positive definite.
All inputs are finite; a program needn't handle non-finite values.
Results may differ from a plain program's by a relative error of at most 0.0004.
Values sent between devices are 32-bit elements; how exact they have to be, the bound alone decides.
A program may use at most 128 MiB of HBM per device.

v0:
```python
import jax
import jax.numpy as jnp
from jax import lax
from jax.sharding import PartitionSpec as P

ITERS = 3


def inner_product(resid, precon_vec):
    return lax.psum(jnp.sum(resid * precon_vec), ("row", "col"))


def per_device(right_side, diag_blocks, precond, tile_values, pair_rows, pair_cols, tile_counts):
    hp = lax.Precision.HIGHEST
    tiles_here = tile_values[0, 0]
    rows_here = pair_rows[0, 0]
    cols_here = pair_cols[0, 0]
    count_here = tile_counts[0, 0]
    per_dev = right_side.shape[0]
    slots = rows_here.shape[0]
    n_row = lax.axis_size("row")
    n_col = lax.axis_size("col")
    row_span = per_dev * n_col
    live = (jnp.arange(slots, dtype=jnp.int32) < count_here).astype(jnp.float32)
    my_row = lax.axis_index("row")
    my_col = lax.axis_index("col")
    total = per_dev * n_row * n_col
    glob_rows = my_row * row_span + rows_here
    glob_cols = cols_here // per_dev * row_span + my_col * per_dev + cols_here % per_dev
    every_tile = jnp.arange(total, dtype=jnp.int32)[None, :]
    row_pick = (glob_rows[:, None] == every_tile).astype(jnp.float32) * live[:, None]
    col_pick = (glob_cols[:, None] == every_tile).astype(jnp.float32) * live[:, None]

    def apply_precond(vec):
        return jnp.einsum("tab,tb->ta", precond, vec, precision=hp)

    solution = jnp.zeros_like(right_side)
    residual = right_side
    precon_r = apply_precond(residual)
    direction = precon_r
    rz_now = inner_product(residual, precon_r)
    for step in range(ITERS):
        local = jnp.einsum("tab,tb->ta", diag_blocks, direction, precision=hp)
        whole = lax.all_gather(direction, ("row", "col"), axis=0, tiled=True)
        fwd = jnp.einsum("sab,sb->sa", tiles_here, whole[glob_cols], precision=hp)
        back = jnp.einsum("sab,sa->sb", tiles_here, whole[glob_rows], precision=hp)
        full = jnp.einsum("sn,sa->na", row_pick, fwd, precision=hp)
        full = full + jnp.einsum("sn,sa->na", col_pick, back, precision=hp)
        image = local + lax.psum_scatter(full, ("row", "col"), scatter_dimension=0, tiled=True)
        alpha = rz_now / lax.psum(jnp.sum(direction * image), ("row", "col"))
        solution = solution + alpha * direction
        residual = residual - alpha * image
        if step + 1 < ITERS:
            precon_r = apply_precond(residual)
            rz_next = inner_product(residual, precon_r)
            direction = precon_r + rz_next / rz_now * direction
            rz_now = rz_next
    return (solution, residual)


def solution(mesh):
    return jax.shard_map(
        per_device,
        mesh=mesh,
        in_specs=(
            P(("row", "col"), None),
            P(("row", "col"), None, None),
            P(("row", "col"), None, None),
            P("row", "col", None, None, None),
            P("row", "col", None),
            P("row", "col", None),
            P("row", "col"),
        ),
        out_specs=(P(("row", "col"), None), P(("row", "col"), None)),
        check_vma=False,
    )
```

profile of v0, /device:TPU:1, one launch (start us, length us, event | category | flops | bytes accessed | tf_op | source)
XLA Modules:
  0.0 1304.3 jit_solution(7082537510070044078)
XLA Ops:
  7.2 0.0 copy-start.5
  7.2 0.0 copy-start.4
  7.2 0.0 all-gather.4.cloned.1.call-start
  7.2 10.6 fusion.69
  17.8 0.6 copy.110
  18.5 0.0 all-gather.4.cloned.1.call-update
  18.5 0.2 reduce-scatter.4.cloned.1.call-start
  19.5 68.6 %all-gather.4.cloned.1.call-done = f32[2048,288]{1,0:T(8,128)} async-done(((f32[16,288]{1,0:T(8,128)}), f32[2048,288]{1,0:T(8,128)}) %all-gather.4.cloned.1.call-update) | async-done | bytes 2359312 | tf_op jit(solution)/shard_map/all_gather | solution.py:44
  88.1 2.5 gather_fusion
  90.6 15.2 %fusion.10 = f32[32,1,288]{2,1,0:T(1,128)S(1)} fusion(f32[1,1,32,288,288]{4,3,2,1,0:T(8,128)} %param.10, f32[32,288,1]{1,0,2:T(8,128)S(1)} %bitcast.138), kind=kOutput, calls=%fused_computation.16 | convolution fusion | flops 31850496 | bytes 10690560 | tf_op jit(solution)/shard_map/sab,sb->sa/dot_general | solution.py:45
  105.8 2.5 gather_fusion.1
  108.3 10.6 fusion.8
  118.9 0.0 copy-start.2
  119.0 2.9 fusion.19
  121.9 0.0 copy-start.3
  121.9 4.7 convolution_add_fusion.2
  126.6 0.0 reduce-scatter.4.cloned.1.call-update
  126.6 0.0 all-gather.6.cloned.1.call-start
  126.6 8.2 fusion.67
  134.9 196.9 %reduce-scatter.4.cloned.1.call-done = f32[16,288]{1,0:T(8,128)} async-done(((f32[2048,288]{1,0:T(8,128)}), f32[16,288]{1,0:T(8,128)}) %reduce-scatter.4.cloned.1.call-update) | async-done | bytes 18448 | tf_op jit(solution)/shard_map/reduce_scatter | solution.py:49
  331.7 1.4 multiply_reduce_fusion.2
  333.1 64.4 %all-reduce = (f32[]{:T(128)}, f32[]{:T(128)}) all-reduce(f32[]{:T(128)} %get-tuple-element.3, f32[]{:T(128)} %get-tuple-element.2), channel_id=1, replica_groups=mesh['row'=8,'col'=16] {'row','col'}, use_global_device_ids=true, to_apply=%region_1.2 | all-reduce | flops 2 | bytes 16 | tf_op jit(solution)/shard_map/psum | solution.py:10
  398.8 0.7 multiply_subtract_fusion.2
  399.5 8.2 fusion.65
  407.7 0.6 fusion.58
  408.4 62.5 %psum.44 = f32[]{:T(128)} all-reduce(f32[]{:T(128)} %fusion.58), channel_id=1, replica_groups=mesh['row'=8,'col'=16] {'row','col'}, use_global_device_ids=true, to_apply=%region_6.7 | all-reduce | flops 1 | bytes 8 | tf_op jit(solution)/shard_map/psum | solution.py:10
  472.2 0.6 bitcast_add_fusion.3
  472.9 0.0 all-gather.6.cloned.1.call-update
  472.9 0.0 reduce-scatter.6.cloned.1.call-start
  472.9 63.4 %all-gather.6.cloned.1.call-done = f32[2048,288]{1,0:T(8,128)} async-done(((f32[16,288]{1,0:T(8,128)}), f32[2048,288]{1,0:T(8,128)}) %all-gather.6.cloned.1.call-update) | async-done | bytes 2359312 | tf_op jit(solution)/shard_map/all_gather | solution.py:44
  536.4 2.5 gather_fusion.2
  538.9 15.6 %fusion.6 = f32[32,1,288]{2,1,0:T(1,128)S(1)} fusion(f32[1,1,32,288,288]{4,3,2,1,0:T(8,128)} %param.10, f32[32,288,1]{1,0,2:T(8,128)S(1)} %bitcast.139), kind=kOutput, calls=%fused_computation.12 | convolution fusion | flops 31850496 | bytes 10690560 | tf_op jit(solution)/shard_map/sab,sb->sa/dot_general | solution.py:45
  554.5 2.5 gather_fusion.3
  557.0 10.6 fusion.4
  567.6 0.0 copy-start
  567.6 2.9 fusion.17
  570.5 4.7 convolution_add_fusion.1
  575.2 0.0 reduce-scatter.6.cloned.1.call-update
  575.2 0.0 all-gather.8.cloned.1.call-start
  575.3 8.2 fusion.63
  583.5 196.8 %reduce-scatter.6.cloned.1.call-done = f32[16,288]{1,0:T(8,128)} async-done(((f32[2048,288]{1,0:T(8,128)}), f32[16,288]{1,0:T(8,128)}) %reduce-scatter.6.cloned.1.call-update) | async-done | bytes 18448 | tf_op jit(solution)/shard_map/reduce_scatter | solution.py:49
  780.3 1.4 multiply_reduce_fusion.1
  781.7 64.3 %psum.45 = f32[]{:T(128)} all-reduce(f32[]{:T(128)} %multiply_reduce_fusion.1), channel_id=1, replica_groups=mesh['row'=8,'col'=16] {'row','col'}, use_global_device_ids=true, to_apply=%region_9.10 | all-reduce | flops 1 | bytes 8 | tf_op jit(solution)/shard_map/psum | solution.py:50
  847.4 0.7 multiply_subtract_fusion.1
  848.1 8.2 fusion.61
  856.3 0.6 fusion.57
  856.9 62.5 %psum.46 = f32[]{:T(128)} all-reduce(f32[]{:T(128)} %fusion.57), channel_id=1, replica_groups=mesh['row'=8,'col'=16] {'row','col'}, use_global_device_ids=true, to_apply=%region_11.12 | all-reduce | flops 1 | bytes 8 | tf_op jit(solution)/shard_map/psum | solution.py:10
  920.8 0.6 bitcast_add_fusion.1
  921.5 0.0 all-gather.8.cloned.1.call-update
  921.5 0.0 reduce-scatter.8.cloned.1.call-start
  921.5 63.4 %all-gather.8.cloned.1.call-done = f32[2048,288]{1,0:T(8,128)} async-done(((f32[16,288]{1,0:T(8,128)}), f32[2048,288]{1,0:T(8,128)}) %all-gather.8.cloned.1.call-update) | async-done | bytes 2359312 | tf_op jit(solution)/shard_map/all_gather | solution.py:44
  985.0 2.5 gather_fusion.4
  987.5 15.4 %fusion.2 = f32[32,1,288]{2,1,0:T(1,128)S(1)} fusion(f32[1,1,32,288,288]{4,3,2,1,0:T(8,128)} %param.10, f32[32,288,1]{1,0,2:T(8,128)S(1)} %bitcast.137), kind=kOutput, calls=%fused_computation.8 | convolution fusion | flops 31850496 | bytes 10690560 | tf_op jit(solution)/shard_map/sab,sb->sa/dot_general | solution.py:45
  1002.9 2.5 gather_fusion.5
  1005.4 10.7 fusion
  1016.1 0.0 copy-start.1
  1016.1 2.9 fusion.15
  1019.0 4.7 convolution_add_fusion
  1023.7 0.0 reduce-scatter.8.cloned.1.call-update
  1023.7 8.2 fusion.59
  1031.9 196.9 %reduce-scatter.8.cloned.1.call-done = f32[16,288]{1,0:T(8,128)} async-done(((f32[2048,288]{1,0:T(8,128)}), f32[16,288]{1,0:T(8,128)}) %reduce-scatter.8.cloned.1.call-update) | async-done | bytes 18448 | tf_op jit(solution)/shard_map/reduce_scatter | solution.py:49
  1228.8 1.3 multiply_reduce_fusion
  1230.1 64.3 %psum.47 = f32[]{:T(128)} all-reduce(f32[]{:T(128)} %multiply_reduce_fusion), channel_id=1, replica_groups=mesh['row'=8,'col'=16] {'row','col'}, use_global_device_ids=true, to_apply=%region_14.15 | all-reduce | flops 1 | bytes 8 | tf_op jit(solution)/shard_map/psum | solution.py:50
  1295.8 1.4 multiply_subtract_fusion
  (13 shorter events, 0.1 us)
Async XLA Ops:
  7.2 12.2 copy-start.5
  7.2 12.2 copy-start.4
  7.2 80.9 %all-gather.4.cloned.1.call-start = ((), (), s32[]{:S(2)}) async-start(), calls=%async_computation.3 | async-start | bytes 3170304 | tf_op jit(solution)/shard_map/all_gather | solution.py:44
  18.5 313.2 %reduce-scatter.4.cloned.1.call-start = ((), (), s32[]{:S(2)}) async-start(), calls=%async_computation.4 | async-start | bytes 3170304 | tf_op jit(solution)/shard_map/reduce_scatter | solution.py:49
  118.9 7.7 copy-start.2
  121.9 209.8 %copy-start.3 = (f32[16,288]{1,0:T(8,128)S(1)}, f32[16,288]{1,0:T(8,128)}, u32[]{:S(2)}) copy-start(f32[16,288]{1,0:T(8,128)} %param.7) | copy-start | bytes 55300
  126.6 409.8 %all-gather.6.cloned.1.call-start = ((), (), s32[]{:S(2)}) async-start(), calls=%async_computation.5 | async-start | bytes 3170304 | tf_op jit(solution)/shard_map/all_gather | solution.py:44
  472.9 307.4 %reduce-scatter.6.cloned.1.call-start = ((), (), s32[]{:S(2)}) async-start(), calls=%async_computation.6 | async-start | bytes 3170304 | tf_op jit(solution)/shard_map/reduce_scatter | solution.py:49
  567.6 7.7 copy-start
  575.2 409.8 %all-gather.8.cloned.1.call-start = ((), (), s32[]{:S(2)}) async-start(), calls=%async_computation.7 | async-start | bytes 3170304 | tf_op jit(solution)/shard_map/all_gather | solution.py:44
  921.5 307.3 %reduce-scatter.8.cloned.1.call-start = ((), (), s32[]{:S(2)}) async-start(), calls=%async_computation.8 | async-start | bytes 3170304 | tf_op jit(solution)/shard_map/reduce_scatter | solution.py:49
  1016.1 7.6 copy-start.1
Sparse Core Ops, SparseCore 0:
  18.6 69.4 all-gather.3
  126.7 204.9 reduce-scatter.3
  473.0 63.3 all-gather.5
  575.3 204.9 reduce-scatter.5
  921.6 63.3 all-gather.7
  1023.8 204.9 reduce-scatter.7
where the time goes:
time: 1310 us; the launch traced here: 1300 us
  waiting for transfers between devices  786 us (60%)
  blocking collectives  318 us (24%)
  matrix products  152 us (12%)
  between operations  22.1 us (2%)
  local copies, waits for them, and re-layouts  15.7 us (1%)
    reduce_scatter x3, waiting for transfers between devices, per_device(): lax.psum_scatter(full, ('row', 'col'), scatter_dimension=0, tiled=True)  591 us
    all_gather x3, waiting for transfers between devices, per_device(): whole = lax.all_gather(direction, ('row', 'col'), axis=0, tiled=True)  196 us
    psum x3, blocking collectives, inner_product(): return lax.psum(jnp.sum(resid * precon_vec), ('row', 'col'))  189 us
    psum x2, blocking collectives, per_device(): alpha = rz_now / lax.psum(jnp.sum(direction * image), ('row', 'col'))  129 us
    dot_general x3, matrix products, per_device(): fwd = jnp.einsum('sab,sb->sa', tiles_here, whole[glob_cols], precision=hp)  46.1 us
    dot_general x3, matrix products, per_device(): back = jnp.einsum('sab,sa->sb', tiles_here, whole[glob_rows], precision=hp)  31.9 us
    dot_general x3, matrix products, apply_precond(): return jnp.einsum('tab,tb->ta', precond, vec, precision=hp)  27 us
  transfers between devices with their start and end apart: 6, of which 6 were waited for; matrix products, arithmetic and copies ran while one was open for 2% of the time, Pallas kernels for 0%

commit v1 on v0

v1 whole, which is shorter than its diff:
```python
import functools

import jax
import jax.numpy as jnp
from jax import lax
from jax.experimental import pallas as pl
from jax.experimental.pallas import tpu as pltpu
from jax.sharding import PartitionSpec as P

ITERS = 3
LANES = 128
MESH = pl.DeviceIdType.MESH
F32 = jnp.float32
BF16 = jnp.bfloat16


def three_parts(value):
    high = value.astype(BF16)
    rest = value - high.astype(F32)
    middle = rest.astype(BF16)
    low = (rest - middle.astype(F32)).astype(BF16)
    return high, middle, low


def apply_blocks(blocks, vec, out, first, last):
    width = blocks.shape[1]
    turned = jnp.transpose(vec)
    for t in range(first, last):
        out[t : t + 1, 0:width] = jnp.sum(blocks[t] * turned[0:width, t : t + 1], axis=0, keepdims=True)


def total(value):
    return jnp.sum(jnp.sum(value, axis=0, keepdims=True), axis=1, keepdims=True)


def kernel(
    n_row, n_col,
    rows_s, cols_s, count_s, rows_v, cols_v, rhs, diag_hbm, prec_hbm, tile_hbm,
    sol_out, res_out,
    tiles, diag, prec,
    msg, got_row0, got_row1, got_row2, got_col0, got_col1, got_col2, sum_row, sum_col, out_row, out_col,
    picked, backs, local, stage, dots, dot_col, dot_row,
    x_v, r_v, p_v, s_v,
    prec_sem, diag_sem, tile_sem,
    msg_col_ssem, msg_row_ssem, got_row_sem, got_col_sem,
    out_row_ssem, out_col_ssem, sum_row_sem, sum_col_sem,
    dot_ssem, dot_rsem,
):
    got_row_of, got_col_of = (got_row0, got_row1, got_row2), (got_col0, got_col1, got_col2)
    per_dev, width = rhs.shape
    slots = tiles.shape[0]
    wide = msg.shape[2]
    spare = wide - LANES
    first_lane = width - spare
    my_row = lax.axis_index("row")
    my_col = lax.axis_index("col")

    part = per_dev // 4
    for k in range(4):
        pltpu.make_async_copy(
            prec_hbm.at[pl.ds(k * part, part)], prec.at[pl.ds(k * part, part)], prec_sem.at[k]
        ).start()
    pltpu.make_async_copy(diag_hbm, diag, diag_sem).start()
    pltpu.make_async_copy(tile_hbm, tiles, tile_sem).start()

    barrier = pltpu.get_barrier_semaphore()

    def greet_col(i, _):
        pl.semaphore_signal(barrier, inc=1, device_id=(my_row, lax.rem(my_col + i, n_col)), device_id_type=MESH)
        return 0

    def greet_row(i, _):
        pl.semaphore_signal(barrier, inc=1, device_id=(lax.rem(my_row + i, n_row), my_col), device_id_type=MESH)
        return 0

    lax.fori_loop(1, n_col, greet_col, 0)
    lax.fori_loop(1, n_row, greet_row, 0)

    def to_cols(source, target, send_sem, recv_sem):
        def step(i, _):
            peer = lax.rem(my_col + i, n_col)
            pltpu.make_async_remote_copy(
                src_ref=source(peer), dst_ref=target, send_sem=send_sem, recv_sem=recv_sem,
                device_id=(my_row, peer), device_id_type=MESH,
            ).start()
            return 0
        lax.fori_loop(1, n_col, step, 0)

    def to_rows(source, target, send_sem, recv_sem):
        def step(i, _):
            peer = lax.rem(my_row + i, n_row)
            pltpu.make_async_remote_copy(
                src_ref=source(peer), dst_ref=target, send_sem=send_sem, recv_sem=recv_sem,
                device_id=(peer, my_col), device_id_type=MESH,
            ).start()
            return 0
        lax.fori_loop(1, n_row, step, 0)

    def wait_bytes(ref, sem):
        pltpu.make_async_copy(ref, ref, sem).wait()

    def block(index):
        return pl.ds(pl.multiple_of(index * per_dev, per_dev), per_dev)

    col_blocks = pl.ds(0, (n_col - 1) * per_dev)
    row_blocks = pl.ds(0, (n_row - 1) * per_dev)

    count = count_s[0, 0]
    slot_lane = lax.broadcasted_iota(jnp.int32, (n_col * per_dev, slots), 1)
    tile_of = lax.broadcasted_iota(jnp.int32, (n_col * per_dev, slots), 0)
    pick_row = ((tile_of == rows_v[...]) & (slot_lane < count)).astype(F32)
    pick_row = jnp.concatenate([pick_row, jnp.zeros((n_col * per_dev, LANES - slots), F32)], axis=1).astype(BF16)
    pick_row = jnp.concatenate([pick_row] * 3, axis=1)
    slot_lane = lax.broadcasted_iota(jnp.int32, (n_row * per_dev, slots), 1)
    tile_of = lax.broadcasted_iota(jnp.int32, (n_row * per_dev, slots), 0)
    pick_col = ((tile_of == cols_v[...]) & (slot_lane < count)).astype(F32)
    pick_col = jnp.concatenate([pick_col] * 3, axis=1).astype(BF16)

    lane = lax.broadcasted_iota(jnp.int32, (per_dev, wide), 1)
    sub = lax.broadcasted_iota(jnp.int32, (per_dev, wide), 0)
    valid = lane < width

    head = lax.broadcasted_iota(jnp.int32, (n_col * per_dev, LANES), 0) % per_dev == 0
    dot_lane = lax.broadcasted_iota(jnp.int32, (8, LANES), 1)

    for ref in (local, stage, backs, x_v, r_v):
        ref[...] = jnp.zeros_like(ref)
    r_v[:, 0:width] = rhs[...]

    residual = r_v[...]
    for k in range(4):
        pltpu.make_async_copy(
            prec_hbm.at[pl.ds(k * part, part)], prec.at[pl.ds(k * part, part)], prec_sem.at[k]
        ).wait()
        apply_blocks(prec, residual, stage, k * part, (k + 1) * part)
    z = stage[...]
    msg[0] = z + jnp.where((sub == 0) & (lane == width), total(residual * z), 0.0)

    pl.semaphore_wait(barrier, n_col + n_row - 2)

    for j in range(ITERS):
        got_row, got_col = got_row_of[j], got_col_of[j]
        to_rows(lambda peer: msg.at[j], got_col.at[block(my_row)], msg_row_ssem.at[j], got_col_sem.at[j])
        to_cols(lambda peer: msg.at[j], got_row.at[block(my_col)], msg_col_ssem.at[j], got_row_sem.at[j])
        vec = msg[j]
        got_col[block(my_row), :] = vec
        got_row[block(my_col), :] = vec
        z = jnp.where(valid, vec, 0.0)

        if j == 0:
            pltpu.make_async_copy(diag_hbm, diag, diag_sem).wait()
        apply_blocks(diag, vec, local, 0, per_dev)
        delta = total(z * local[...])

        if j == 0:
            pltpu.make_async_copy(tile_hbm, tiles, tile_sem).wait()
        wait_bytes(got_col.at[row_blocks], got_col_sem.at[j])
        turned_lane = lax.broadcasted_iota(jnp.int32, (width, LANES), 1)
        products = jnp.zeros((width, LANES), F32)
        for slot in range(slots):
            index = jnp.clip(cols_s[0, slot], 0, n_row * per_dev - 1)
            product = jnp.sum(tiles[slot] * got_col[pl.ds(index, 1), 0:width], axis=1, keepdims=True)
            products = jnp.where(turned_lane == slot, product, products)
        products = jnp.where(turned_lane < count, products, 0.0)
        filled = jnp.concatenate([products, jnp.zeros((wide - width, LANES), F32)], axis=0)
        out_row[j] = lax.dot_general(
            pick_row, jnp.concatenate(three_parts(filled), axis=1),
            (((1,), (1,)), ((), ())), preferred_element_type=F32,
        )
        to_cols(lambda peer: out_row.at[j, block(peer)], sum_row.at[j, block(my_col)], out_row_ssem.at[j], sum_row_sem.at[j])
        sum_row[j, block(my_col), :] = out_row[j, block(my_col), :]

        wait_bytes(got_row.at[col_blocks], got_row_sem.at[j])
        for slot in range(slots):
            index = jnp.clip(rows_s[0, slot], 0, n_col * per_dev - 1)
            picked[slot : slot + 1, :] = got_row[pl.ds(index, 1), :]
        turned = jnp.transpose(picked[...])
        delta = delta + 2.0 * total(products[:, 0:slots] * turned[0:width, :])
        partial = jnp.sum(jnp.where(head, got_row[:, spare:wide], 0.0), axis=0, keepdims=True)
        dots[j, 0] = jnp.where(dot_lane == 0, delta, jnp.where(dot_lane >= first_lane, partial, 0.0))
        to_rows(lambda peer: dots.at[j, 0], dot_col.at[j, my_row], dot_ssem.at[j, 0], dot_rsem.at[j, 0])
        dot_col[j, my_row] = dots[j, 0]

        for slot in range(slots):
            backs[slot : slot + 1, 0:width] = jnp.sum(
                tiles[slot] * turned[0:width, slot : slot + 1], axis=0, keepdims=True
            )
        live = lax.broadcasted_iota(jnp.int32, (slots, wide), 0) < count
        out_col[j] = jnp.dot(
            pick_col, jnp.concatenate(three_parts(jnp.where(live, backs[...], 0.0)), axis=0),
            preferred_element_type=F32,
        )
        to_rows(lambda peer: out_col.at[j, block(peer)], sum_col.at[j, block(my_row)], out_col_ssem.at[j], sum_col_sem.at[j])
        sum_col[j, block(my_row), :] = out_col[j, block(my_row), :]

        wait_bytes(dot_col.at[j, pl.ds(0, n_row - 1)], dot_rsem.at[j, 0])
        sums = jnp.sum(dot_col[j], axis=0)
        dots[j, 1] = sums
        to_cols(lambda peer: dots.at[j, 1], dot_row.at[j, my_col], dot_ssem.at[j, 1], dot_rsem.at[j, 1])
        dot_row[j, my_col] = sums
        gamma = sums[0:1, first_lane : first_lane + 1]
        cross = sums[0:1, first_lane + 1 : first_lane + 2]

        wait_bytes(sum_col.at[j, row_blocks], sum_col_sem.at[j])
        image = local[...]
        for k in range(n_row):
            image = image + sum_col[j, k * per_dev : (k + 1) * per_dev, :]
        wait_bytes(sum_row.at[j, col_blocks], sum_row_sem.at[j])
        for k in range(n_col):
            image = image + sum_row[j, k * per_dev : (k + 1) * per_dev, :]

        wait_bytes(dot_row.at[j, pl.ds(0, n_col - 1)], dot_rsem.at[j, 1])
        curve = jnp.sum(dot_row[j], axis=0)[0:1, 0:1]
        if j > 0:
            beta = gamma / old_gamma
            curve = curve + beta * (cross + beta * old_curve)
            z = z + beta * p_v[...]
            image = image + beta * s_v[...]
        alpha = gamma / curve
        old_gamma, old_curve = gamma, curve
        x_v[...] = x_v[...] + alpha * z
        r_v[...] = r_v[...] - alpha * image

        if j < ITERS - 1:
            p_v[...] = z
            s_v[...] = image
            residual = r_v[...]
            apply_blocks(prec, residual, stage, 0, per_dev)
            z = stage[...]
            aside = jnp.where(lane == width, total(residual * z), 2.0 * total(z * image))
            msg[j + 1] = z + jnp.where((sub == 0) & (lane >= width) & (lane < width + 2), aside, 0.0)

    sol_out[...] = x_v[:, 0:width]
    res_out[...] = r_v[:, 0:width]

    for j in range(ITERS):
        wait_bytes(got_col_of[j].at[row_blocks], msg_row_ssem.at[j])
        wait_bytes(got_row_of[j].at[col_blocks], msg_col_ssem.at[j])
        wait_bytes(sum_row.at[j, col_blocks], out_row_ssem.at[j])
        wait_bytes(sum_col.at[j, row_blocks], out_col_ssem.at[j])
        wait_bytes(dot_col.at[j, pl.ds(0, n_row - 1)], dot_ssem.at[j, 0])
        wait_bytes(dot_row.at[j, pl.ds(0, n_col - 1)], dot_ssem.at[j, 1])


def per_device(right_side, diag_blocks, precond, tile_values, pair_rows, pair_cols, tile_counts):
    n_row = lax.axis_size("row")
    n_col = lax.axis_size("col")
    per_dev, width = right_side.shape
    slots = tile_values.shape[2]
    wide = -(-(width + 2) // LANES) * LANES
    rows_here = pair_rows[0]
    cols_here = pair_cols[0]
    smem = pl.BlockSpec(memory_space=pltpu.SMEM)
    vmem = pl.BlockSpec(memory_space=pltpu.VMEM)
    anywhere = pl.BlockSpec(memory_space=pl.ANY)
    vector = pltpu.VMEM((per_dev, wide), F32)
    row_area = pltpu.VMEM((ITERS, n_col * per_dev, wide), F32)
    col_area = pltpu.VMEM((ITERS, n_row * per_dev, wide), F32)
    got_rows = [pltpu.VMEM((n_col * per_dev, wide), F32)] * ITERS
    got_cols = [pltpu.VMEM((n_row * per_dev, wide), F32)] * ITERS
    each = pltpu.SemaphoreType.DMA((ITERS,))
    return pl.pallas_call(
        functools.partial(kernel, n_row, n_col),
        out_shape=(jax.ShapeDtypeStruct((per_dev, width), F32),) * 2,
        in_specs=[smem, smem, smem, vmem, vmem, vmem, anywhere, anywhere, anywhere],
        out_specs=(vmem, vmem),
        scratch_shapes=[
            pltpu.VMEM((slots, width, width), F32),
            pltpu.VMEM((per_dev, width, width), F32),
            pltpu.VMEM((per_dev, width, width), F32),
            pltpu.VMEM((ITERS, per_dev, wide), F32),
            *got_rows, *got_cols, row_area, col_area, row_area, col_area,
            pltpu.VMEM((slots, wide), F32),
            pltpu.VMEM((slots, wide), F32),
            vector, vector,
            pltpu.VMEM((ITERS, 2, 8, LANES), F32),
            pltpu.VMEM((ITERS, n_row, 8, LANES), F32),
            pltpu.VMEM((ITERS, n_col, 8, LANES), F32),
            vector, vector, vector, vector,
            pltpu.SemaphoreType.DMA((4,)),
            pltpu.SemaphoreType.DMA,
            pltpu.SemaphoreType.DMA,
            each, each, each, each, each, each, each, each,
            pltpu.SemaphoreType.DMA((ITERS, 2)),
            pltpu.SemaphoreType.DMA((ITERS, 2)),
        ],
        compiler_params=pltpu.CompilerParams(
            collective_id=0, has_side_effects=True, vmem_limit_bytes=56 * 2**20
        ),
    )(
        rows_here, cols_here, tile_counts, rows_here, cols_here,
        right_side, diag_blocks, precond, tile_values[0, 0],
    )


def solution(mesh):
    return jax.shard_map(
        per_device,
        mesh=mesh,
        in_specs=(
            P(("row", "col"), None),
            P(("row", "col"), None, None),
            P(("row", "col"), None, None),
            P("row", "col", None, None, None),
            P("row", "col", None),
            P("row", "col", None),
            P("row", "col"),
        ),
        out_specs=(P(("row", "col"), None), P(("row", "col"), None)),
        check_vma=False,
    )
```

time: 1310 us -> 65.6 us (0.05)
  waiting for transfers between devices: 786 us -> 0 us
  blocking collectives: 318 us -> 0 us
  matrix products: 152 us -> 0 us
  Pallas kernels: 0 us -> 61.3 us
  between operations: 22.1 us -> 1.29 us
    reduce_scatter x3 -> x0, waiting for transfers between devices: 591 us -> none  [per_device(): lax.psum_scatter(full, ('row', 'col'), scatter_dimension=0, tiled=True)]
    psum x5 -> x0, blocking collectives: 318 us -> none  [the longest x3 189 us: inner_product(): return lax.psum(jnp.sum(resid * precon_vec), ('row', 'col'))]
    all_gather x3 -> x0, waiting for transfers between devices: 196 us -> none  [per_device(): whole = lax.all_gather(direction, ('row', 'col'), axis=0, tiled=True)]
    dot_general x18 -> x0, matrix products: 152 us -> none  [the longest x3 46.1 us: per_device(): fwd = jnp.einsum('sab,sb->sa', tiles_here, whole[glob_cols], precision=hp)]
    pallas_call x0 -> x1, Pallas kernels: none -> 61.3 us  [per_device(): pl.pallas_call(functools.partial(kernel, n_row, n_col), out_shape=(jax.Sh...]
    gather x6 -> x0, local copies, waits for them, and re-layouts: 15.1 us -> none  [the longest x3 7.56 us: per_device(): back = jnp.einsum('sab,sa->sb', tiles_here, whole[glob_rows], precision=hp)]
  transfers between devices with their start and end apart: 6 -> 0, of which waited for: 6 -> 0; matrix products, arithmetic and copies ran while one was open for 2% -> 0% of each run, Pallas kernels for 0% -> 0%
where the time goes in v1:
time: 65.6 us; the launch traced here: 65.3 us
  Pallas kernels  61.3 us (93%)
  local copies, waits for them, and re-layouts  2.69 us (4%)
  between operations  1.29 us (2%)
    pallas_call x1, Pallas kernels, per_device(): pl.pallas_call(functools.partial(kernel, n_row, n_col), out_shape=(jax.Sh...  61.3 us
    unnamed x2, local copies, waits for them, and re-layouts  2.69 us

profile of v1, /device:TPU:1, one launch (start us, length us, event | category | flops | bytes accessed | tf_op | source)
XLA Modules:
  0.0 65.3 jit_solution(899394211812503527)
XLA Ops:
  1.3 61.3 %shard_map.86 = (f32[16,288]{1,0:T(8,128)}, f32[16,288]{1,0:T(8,128)}) custom-call(s32[1,32]{1,0:T(1,128)} %bitcast.4, s32[1,32]{1,0:T(1,128)} %bitcast.6, s32[1,1]{1,0:T(1,128)S(6)} %copy.11.count_s, s32[1,32]{1,0:T(1,128)} %bitcast.5, s32[1,32]{1,0:T(1,128)} %bitcast.7, f32[16,288]{1,0:T(8,128)} %rhs.1, f32[16,288,288]{2,1,0:T(8,128)} %diag_hbm.1, ...), custom_call_target="tpu_custom_call" | custom-call | tf_op jit(solution)/shard_map/pallas_call | solution.py:262
  62.6 1.3 %copy.12 = f32[16,288]{1,0:T(8,128)} copy(f32[16,288]{1,0:T(8,128)} %get-tuple-element.4) | data formatting | bytes 36864
  63.9 1.3 %copy.13 = f32[16,288]{1,0:T(8,128)} copy(f32[16,288]{1,0:T(8,128)} %get-tuple-element.5) | data formatting | bytes 36864

commit v2 on v1

v2 whole, which is shorter than its diff:
```python
import functools

import jax
import jax.numpy as jnp
from jax import lax
from jax.experimental import pallas as pl
from jax.experimental.pallas import tpu as pltpu
from jax.sharding import PartitionSpec as P

ITERS = 3
LANES = 128
MESH = pl.DeviceIdType.MESH
F32 = jnp.float32
BF16 = jnp.bfloat16


def three_parts(value):
    high = value.astype(BF16)
    rest = value - high.astype(F32)
    middle = rest.astype(BF16)
    low = (rest - middle.astype(F32)).astype(BF16)
    return high, middle, low


def apply_blocks(blocks, vec, out, first, last):
    width = blocks.shape[1]
    turned = jnp.transpose(vec)
    for t in range(first, last):
        out[t : t + 1, 0:width] = jnp.sum(blocks[t] * turned[0:width, t : t + 1], axis=0, keepdims=True)


def total(value):
    return jnp.sum(jnp.sum(value, axis=0, keepdims=True), axis=1, keepdims=True)


def kernel(
    n_row, n_col,
    rows_s, cols_s, count_s, rows_v, cols_v, rhs, diag_hbm, prec_hbm, tile_hbm,
    both_out,
    tiles, diag, prec,
    msg, got_row0, got_row1, got_row2, got_col0, got_col1, got_col2, sum_row, sum_col, out_row, out_col,
    picked, backs, local, dots, dot_col, dot_row,
    x_v, rh_v, z_v, w_v, r_v, s_v, p_v,
    prec_sem, diag_sem, tile_sem,
    msg_col_ssem, msg_row_ssem, got_row_sem, got_col_sem,
    out_row_ssem, out_col_ssem, sum_row_sem, sum_col_sem,
    dot_ssem, dot_rsem,
):
    got_row_of, got_col_of = (got_row0, got_row1, got_row2), (got_col0, got_col1, got_col2)
    per_dev, width = rhs.shape
    slots = tiles.shape[0]
    wide = msg.shape[2]
    my_row = lax.axis_index("row")
    my_col = lax.axis_index("col")

    part = per_dev // 4
    for k in range(4):
        pltpu.make_async_copy(
            prec_hbm.at[pl.ds(k * part, part)], prec.at[pl.ds(k * part, part)], prec_sem.at[k]
        ).start()
    pltpu.make_async_copy(diag_hbm, diag, diag_sem).start()
    pltpu.make_async_copy(tile_hbm, tiles, tile_sem).start()

    barrier = pltpu.get_barrier_semaphore()

    side = 4
    my_z, my_y = my_col // side, my_col % side
    my_x, my_core = my_row // 2, my_row % 2
    far = (2, 1, 3, 0)
    col_peers = [
        lax.rem(my_z + dz, side) * side + lax.rem(my_y + dy, side)
        for dz, dy in sorted(
            ((dz, dy) for dz in far for dy in far if dz or dy),
            key=lambda d: -(min(d[0], side - d[0]) + min(d[1], side - d[1])),
        )
    ]
    row_peers = [
        lax.rem(my_x + dx, side) * 2 + lax.rem(my_core + dc, 2)
        for dx in far for dc in (0, 1) if dx or dc
    ]

    for peer in col_peers:
        pl.semaphore_signal(barrier, inc=1, device_id=(my_row, peer), device_id_type=MESH)
    for peer in row_peers:
        pl.semaphore_signal(barrier, inc=1, device_id=(peer, my_col), device_id_type=MESH)

    def to_cols(source, target, send_sem, recv_sem):
        for peer in col_peers:
            pltpu.make_async_remote_copy(
                src_ref=source(peer), dst_ref=target, send_sem=send_sem, recv_sem=recv_sem,
                device_id=(my_row, peer), device_id_type=MESH,
            ).start()

    def to_rows(source, target, send_sem, recv_sem):
        for peer in row_peers:
            pltpu.make_async_remote_copy(
                src_ref=source(peer), dst_ref=target, send_sem=send_sem, recv_sem=recv_sem,
                device_id=(peer, my_col), device_id_type=MESH,
            ).start()

    def wait_bytes(ref, sem):
        pltpu.make_async_copy(ref, ref, sem).wait()

    def block(index):
        return pl.ds(pl.multiple_of(index * per_dev, per_dev), per_dev)

    col_blocks = pl.ds(0, (n_col - 1) * per_dev)
    row_blocks = pl.ds(0, (n_row - 1) * per_dev)

    count = count_s[0, 0]
    slot_lane = lax.broadcasted_iota(jnp.int32, (n_col * per_dev, slots), 1)
    tile_of = lax.broadcasted_iota(jnp.int32, (n_col * per_dev, slots), 0)
    pick_row = ((tile_of == rows_v[...]) & (slot_lane < count)).astype(F32)
    pick_row = jnp.concatenate([pick_row, jnp.zeros((n_col * per_dev, LANES - slots), F32)], axis=1).astype(BF16)
    pick_row = jnp.concatenate([pick_row] * 3, axis=1)
    slot_lane = lax.broadcasted_iota(jnp.int32, (n_row * per_dev, slots), 1)
    tile_of = lax.broadcasted_iota(jnp.int32, (n_row * per_dev, slots), 0)
    pick_col = ((tile_of == cols_v[...]) & (slot_lane < count)).astype(F32)
    pick_col = jnp.concatenate([pick_col] * 3, axis=1).astype(BF16)

    dot_lane = lax.broadcasted_iota(jnp.int32, (8, LANES), 1)

    for ref in (local, backs, x_v, rh_v, msg):
        ref[...] = jnp.zeros_like(ref)
    rh_v[:, 0:width] = rhs[...]

    residual = rh_v[...]
    for k in range(4):
        pltpu.make_async_copy(
            prec_hbm.at[pl.ds(k * part, part)], prec.at[pl.ds(k * part, part)], prec_sem.at[k]
        ).wait()
        apply_blocks(prec, residual, msg.at[0], k * part, (k + 1) * part)

    pl.semaphore_wait(barrier, n_col + n_row - 2)

    def small(j, k, along_row):
        if along_row:
            target, me, send = dot_row.at[j, k], my_col, to_cols
        else:
            target, me, send = dot_col.at[j, k], my_row, to_rows
        send(lambda peer: dots.at[j, k], target.at[me], dot_ssem.at[j, k], dot_rsem.at[j, k])
        target[me] = dots[j, k]

    def small_sum(j, k, along_row):
        source, peers = (dot_row, n_col - 1) if along_row else (dot_col, n_row - 1)
        wait_bytes(source.at[j, k, pl.ds(0, peers)], dot_rsem.at[j, k])
        return jnp.sum(source[j, k], axis=0)

    def in_lanes(*values):
        packed = jnp.zeros((8, LANES), F32)
        for k, value in enumerate(values):
            packed = jnp.where(dot_lane == k, value, packed)
        return packed

    def lanes_of(packed, n):
        return [packed[0:1, k : k + 1] for k in range(n)]

    for j in range(ITERS):
        last = j == ITERS - 1
        got_row, got_col = got_row_of[j], got_col_of[j]
        to_rows(lambda peer: msg.at[j], got_col.at[block(my_row)], msg_row_ssem.at[j], got_col_sem.at[j])
        to_cols(lambda peer: msg.at[j], got_row.at[block(my_col)], msg_col_ssem.at[j], got_row_sem.at[j])
        zh = msg[j]
        rh = rh_v[...]
        got_col[block(my_row), :] = zh
        got_row[block(my_col), :] = zh

        if j == 0:
            pltpu.make_async_copy(diag_hbm, diag, diag_sem).wait()
        apply_blocks(diag, zh, local, 0, per_dev)
        own = zh * local[...]
        early = [total(own), total(rh * zh)]
        if j > 0:
            z, w, r, s = z_v[...], w_v[...], r_v[...], s_v[...]
            early += [total(rh * z + r * zh), total(zh * w), total(zh * s), total(z * s)]
        dots[j, 0] = in_lanes(*early)
        small(j, 0, True)

        if j == 0:
            pltpu.make_async_copy(tile_hbm, tiles, tile_sem).wait()
        wait_bytes(got_col.at[row_blocks], got_col_sem.at[j])
        turned_lane = lax.broadcasted_iota(jnp.int32, (width, LANES), 1)
        products = jnp.zeros((width, LANES), F32)
        for slot in range(slots):
            index = jnp.clip(cols_s[0, slot], 0, n_row * per_dev - 1)
            product = jnp.sum(tiles[slot] * got_col[pl.ds(index, 1), 0:width], axis=1, keepdims=True)
            products = jnp.where(turned_lane == slot, product, products)
        products = jnp.where(turned_lane < count, products, 0.0)
        products = jnp.concatenate([products, jnp.zeros((wide - width, LANES), F32)], axis=0)
        products = lax.dot_general(
            pick_row, jnp.concatenate(three_parts(products), axis=1),
            (((1,), (1,)), ((), ())), preferred_element_type=F32,
        )
        out_row[j] = products

        def send_out_row():
            to_cols(lambda peer: out_row.at[j, block(peer)], sum_row.at[j, block(my_col)], out_row_ssem.at[j], sum_row_sem.at[j])
            sum_row[j, block(my_col), :] = out_row[j, block(my_col), :]

        if not last:
            send_out_row()

        wait_bytes(got_row.at[col_blocks], got_row_sem.at[j])
        shared = jnp.sum((out_row[j] * got_row[...]).reshape(n_col, per_dev, wide), axis=0)
        dots[j, 2] = in_lanes(total(own + 2.0 * shared))
        small(j, 2, last)
        if last:
            send_out_row()
        dots[j, 1] = small_sum(j, 0, True)
        small(j, 1, False)

        for slot in range(slots):
            index = jnp.clip(rows_s[0, slot], 0, n_col * per_dev - 1)
            picked[slot : slot + 1, :] = got_row[pl.ds(index, 1), :]
        turned = jnp.transpose(picked[...])
        for slot in range(slots):
            backs[slot : slot + 1, 0:width] = jnp.sum(
                tiles[slot] * turned[0:width, slot : slot + 1], axis=0, keepdims=True
            )
        live = lax.broadcasted_iota(jnp.int32, (slots, wide), 0) < count
        out_col[j] = jnp.dot(
            pick_col, jnp.concatenate(three_parts(jnp.where(live, backs[...], 0.0)), axis=0),
            preferred_element_type=F32,
        )
        to_rows(lambda peer: out_col.at[j, block(peer)], sum_col.at[j, block(my_row)], out_col_ssem.at[j], sum_col_sem.at[j])
        sum_col[j, block(my_row), :] = out_col[j, block(my_row), :]

        dots[j, 3] = small_sum(j, 2, last)
        small(j, 3, not last)

        if j == 0:
            curve_h, gamma = lanes_of(small_sum(j, 1, False), 2)
            predicted = gamma / curve_h
            z, r = zh, rh
            p = z
        else:
            curve_h, gamma_h, gamma_x, zh_w, zh_s, z_s = lanes_of(small_sum(j, 1, False), 6)
            delta_h = lanes_of(small_sum(j - 1, 3, True), 1)[0]
            if j == 1:
                delta = curve = delta_h
            else:
                delta = rest * (rest * delta_h + twice) + theta * theta * delta
                curve = delta + beta * (cross + beta * curve)
            alpha = gamma / curve
            theta = (predicted - alpha) / predicted
            rest = 1.0 - theta
            beta = (rest * (rest * gamma_h + theta * gamma_x) + theta * theta * gamma) / gamma
            gamma = beta * gamma
            cross = 2.0 * (rest * zh_s + theta * z_s)
            twice = 2.0 * theta * zh_w
            predicted = gamma_h / curve_h
            x_v[...] = x_v[...] + alpha * p_v[...]
            z = rest * zh + theta * z
            r = rest * rh + theta * r
            p = z + beta * p_v[...]
            kept_w = theta * w
            kept_s = beta * s

        wait_bytes(sum_col.at[j, row_blocks], sum_col_sem.at[j])
        image = local[...]
        for k in range(n_row):
            image = image + sum_col[j, k * per_dev : (k + 1) * per_dev, :]
        wait_bytes(sum_row.at[j, col_blocks], sum_row_sem.at[j])
        for k in range(n_col):
            image = image + sum_row[j, k * per_dev : (k + 1) * per_dev, :]
        w = image if j == 0 else rest * image + kept_w
        s = w if j == 0 else w + kept_s
        if not last:
            rh = r - predicted * s
            rh_v[...] = rh
            apply_blocks(prec, rh, msg.at[j + 1], 0, per_dev)
            z_v[...], w_v[...], r_v[...], s_v[...], p_v[...] = z, w, r, s, p

    delta_h = lanes_of(small_sum(ITERS - 1, 3, False), 1)[0]
    delta = rest * (rest * delta_h + twice) + theta * theta * delta
    alpha = gamma / (delta + beta * (cross + beta * curve))
    x = x_v[...] + alpha * p
    r = r - alpha * s
    both_out[0] = x[:, 0:width]
    both_out[1] = r[:, 0:width]

    for j in range(ITERS):
        wait_bytes(got_col_of[j].at[row_blocks], msg_row_ssem.at[j])
        wait_bytes(got_row_of[j].at[col_blocks], msg_col_ssem.at[j])
        wait_bytes(sum_row.at[j, col_blocks], out_row_ssem.at[j])
        wait_bytes(sum_col.at[j, row_blocks], out_col_ssem.at[j])
        for k in range(4):
            along_row = k == 0 or (k == 2) == (j == ITERS - 1) and k > 1
            source, peers = (dot_row, n_col - 1) if along_row else (dot_col, n_row - 1)
            wait_bytes(source.at[j, k, pl.ds(0, peers)], dot_ssem.at[j, k])


def part_kernel(both, sol_out, res_out):
    sol_out[...] = both[0]
    res_out[...] = both[1]


def per_device(right_side, diag_blocks, precond, tile_values, pair_rows, pair_cols, tile_counts):
    n_row = lax.axis_size("row")
    n_col = lax.axis_size("col")
    per_dev, width = right_side.shape
    slots = tile_values.shape[2]
    wide = -(-width // LANES) * LANES
    rows_here = pair_rows[0]
    cols_here = pair_cols[0]
    smem = pl.BlockSpec(memory_space=pltpu.SMEM)
    vmem = pl.BlockSpec(memory_space=pltpu.VMEM)
    anywhere = pl.BlockSpec(memory_space=pl.ANY)
    vector = pltpu.VMEM((per_dev, wide), F32)
    row_area = pltpu.VMEM((ITERS, n_col * per_dev, wide), F32)
    col_area = pltpu.VMEM((ITERS, n_row * per_dev, wide), F32)
    got_rows = [pltpu.VMEM((n_col * per_dev, wide), F32)] * ITERS
    got_cols = [pltpu.VMEM((n_row * per_dev, wide), F32)] * ITERS
    each = pltpu.SemaphoreType.DMA((ITERS,))
    both = pl.pallas_call(
        functools.partial(kernel, n_row, n_col),
        out_shape=jax.ShapeDtypeStruct((2, per_dev, width), F32),
        in_specs=[smem, smem, smem, vmem, vmem, vmem, anywhere, anywhere, anywhere],
        out_specs=vmem,
        scratch_shapes=[
            pltpu.VMEM((slots, width, width), F32),
            pltpu.VMEM((per_dev, width, width), F32),
            pltpu.VMEM((per_dev, width, width), F32),
            pltpu.VMEM((ITERS, per_dev, wide), F32),
            *got_rows, *got_cols, row_area, col_area, row_area, col_area,
            pltpu.VMEM((slots, wide), F32),
            pltpu.VMEM((slots, wide), F32),
            vector,
            pltpu.VMEM((ITERS, 4, 8, LANES), F32),
            pltpu.VMEM((ITERS, 4, n_row, 8, LANES), F32),
            pltpu.VMEM((ITERS, 4, n_col, 8, LANES), F32),
            vector, vector, vector, vector, vector, vector, vector,
            pltpu.SemaphoreType.DMA((4,)),
            pltpu.SemaphoreType.DMA,
            pltpu.SemaphoreType.DMA,
            each, each, each, each, each, each, each, each,
            pltpu.SemaphoreType.DMA((ITERS, 4)),
            pltpu.SemaphoreType.DMA((ITERS, 4)),
        ],
        compiler_params=pltpu.CompilerParams(
            collective_id=0, has_side_effects=True, vmem_limit_bytes=56 * 2**20
        ),
    )(
        rows_here, cols_here, tile_counts, rows_here, cols_here,
        right_side, diag_blocks, precond, tile_values[0, 0],
    )
    return pl.pallas_call(
        part_kernel,
        out_shape=(jax.ShapeDtypeStruct((per_dev, width), F32),) * 2,
        in_specs=[vmem],
        out_specs=(vmem, vmem),
    )(both)


def solution(mesh):
    return jax.shard_map(
        per_device,
        mesh=mesh,
        in_specs=(
            P(("row", "col"), None),
            P(("row", "col"), None, None),
            P(("row", "col"), None, None),
            P("row", "col", None, None, None),
            P("row", "col", None),
            P("row", "col", None),
            P("row", "col"),
        ),
        out_specs=(P(("row", "col"), None), P(("row", "col"), None)),
        check_vma=False,
    )
```

time: 65.6 us -> 61.1 us (0.931)
  local copies, waits for them, and re-layouts: 2.69 us -> 0 us
  Pallas kernels: 61.3 us -> 59.5 us
    unnamed x2 -> x0, local copies, waits for them, and re-layouts: 2.69 us -> none
    pallas_call x1 -> x2, Pallas kernels: 61.3 us -> 59.5 us  [the longest x1 58.1 us: per_device(): pl.pallas_call(functools.partial(kernel, n_row, n_col), out_shape=jax.Sha...]
where the time goes in v2:
time: 61.1 us; the launch traced here: 60.8 us
  Pallas kernels  59.5 us (97%)
  between operations  1.29 us (2%)
    pallas_call x1, Pallas kernels, per_device(): pl.pallas_call(functools.partial(kernel, n_row, n_col), out_shape=jax.Sha...  58.1 us
    pallas_call x1, Pallas kernels, per_device(): pl.pallas_call(part_kernel, out_shape=(jax.ShapeDtypeStruct((per_dev, wid...  1.42 us

profile of v2, /device:TPU:1, one launch (start us, length us, event | category | flops | bytes accessed | tf_op | source)
XLA Modules:
  0.0 60.8 jit_solution(10642210794892304733)
XLA Ops:
  1.3 58.1 %shard_map.86.both = f32[2,16,288]{2,1,0:T(8,128)} custom-call(s32[1,32]{1,0:T(1,128)} %bitcast.4, s32[1,32]{1,0:T(1,128)} %bitcast.6, s32[1,1]{1,0:T(1,128)S(6)} %copy.9.count_s, s32[1,32]{1,0:T(1,128)} %bitcast.5, s32[1,32]{1,0:T(1,128)} %bitcast.7, f32[16,288]{1,0:T(8,128)} %rhs.1, f32[16,288,288]{2,1,0:T(8,128)} %diag_hbm.1, f32[16,288,288]{2,1,0:T(8,128)} %prec_hbm.1, ...), custom_call_target="tpu_custom_call" | custom-call | tf_op jit(solution)/shard_map/pallas_call | solution.py:315
  59.4 1.4 %shard_map.87 = (f32[16,288]{1,0:T(8,128)}, f32[16,288]{1,0:T(8,128)}) custom-call(f32[2,16,288]{2,1,0:T(8,128)} %shard_map.86.both), custom_call_target="tpu_custom_call" | custom-call | tf_op jit(solution)/shard_map/pallas_call | solution.py:347

commit v3 on v2

--- a/solution.py
+++ b/solution.py
@@ -39,7 +39,7 @@
     both_out,
     tiles, diag, prec,
     msg, got_row0, got_row1, got_row2, got_col0, got_col1, got_col2, sum_row, sum_col, out_row, out_col,
-    picked, backs, local, dots, dot_col, dot_row,
+    picked, backs, col_ends, row_ends, local, stage, turn, dots, dot_col, dot_row,
     x_v, rh_v, z_v, w_v, r_v, s_v, p_v,
     prec_sem, diag_sem, tile_sem,
     msg_col_ssem, msg_row_ssem, got_row_sem, got_col_sem,
@@ -49,17 +49,9 @@
     got_row_of, got_col_of = (got_row0, got_row1, got_row2), (got_col0, got_col1, got_col2)
     per_dev, width = rhs.shape
     slots = tiles.shape[0]
-    wide = msg.shape[2]
+    wide = stage.shape[1]
     my_row = lax.axis_index("row")
     my_col = lax.axis_index("col")
-
-    part = per_dev // 4
-    for k in range(4):
-        pltpu.make_async_copy(
-            prec_hbm.at[pl.ds(k * part, part)], prec.at[pl.ds(k * part, part)], prec_sem.at[k]
-        ).start()
-    pltpu.make_async_copy(diag_hbm, diag, diag_sem).start()
-    pltpu.make_async_copy(tile_hbm, tiles, tile_sem).start()
 
     barrier = pltpu.get_barrier_semaphore()
 
@@ -84,6 +76,14 @@
     for peer in row_peers:
         pl.semaphore_signal(barrier, inc=1, device_id=(peer, my_col), device_id_type=MESH)
 
+    part = per_dev // 4
+    for k in range(4):
+        pltpu.make_async_copy(
+            prec_hbm.at[pl.ds(k * part, part)], prec.at[pl.ds(k * part, part)], prec_sem.at[k]
+        ).start()
+    pltpu.make_async_copy(diag_hbm, diag, diag_sem).start()
+    pltpu.make_async_copy(tile_hbm, tiles, tile_sem).start()
+
     def to_cols(source, target, send_sem, recv_sem):
         for peer in col_peers:
             pltpu.make_async_remote_copy(
@@ -101,26 +101,54 @@
     def wait_bytes(ref, sem):
         pltpu.make_async_copy(ref, ref, sem).wait()
 
-    def block(index):
-        return pl.ds(pl.multiple_of(index * per_dev, per_dev), per_dev)
-
-    col_blocks = pl.ds(0, (n_col - 1) * per_dev)
-    row_blocks = pl.ds(0, (n_row - 1) * per_dev)
+    full = width // LANES
+    rest_lanes = width - full * LANES
+    groups = LANES // rest_lanes
+    quarter = per_dev // groups
+    body = full * per_dev
+
+    def pack(value, target):
+        for k in range(full):
+            target[k * per_dev : (k + 1) * per_dev, :] = value[:, k * LANES : (k + 1) * LANES]
+        ends = value[:, full * LANES :]
+        packed = ends[0:quarter, :]
+        for a in range(1, groups):
+            packed = packed + pltpu.roll(ends, a * rest_lanes, 1)[a * quarter : (a + 1) * quarter, :]
+        target[body:, :] = packed
+
+    def spread(packed, target, first):
+        for a in range(groups):
+            row = first + a * quarter
+            target[row : row + quarter, :] = pltpu.roll(packed, LANES - a * rest_lanes, 1) if a else packed
+
+    col_blocks = pl.ds(0, n_col - 1)
+    row_blocks = pl.ds(0, n_row - 1)
 
     count = count_s[0, 0]
-    slot_lane = lax.broadcasted_iota(jnp.int32, (n_col * per_dev, slots), 1)
-    tile_of = lax.broadcasted_iota(jnp.int32, (n_col * per_dev, slots), 0)
-    pick_row = ((tile_of == rows_v[...]) & (slot_lane < count)).astype(F32)
-    pick_row = jnp.concatenate([pick_row, jnp.zeros((n_col * per_dev, LANES - slots), F32)], axis=1).astype(BF16)
-    pick_row = jnp.concatenate([pick_row] * 3, axis=1)
-    slot_lane = lax.broadcasted_iota(jnp.int32, (n_row * per_dev, slots), 1)
-    tile_of = lax.broadcasted_iota(jnp.int32, (n_row * per_dev, slots), 0)
-    pick_col = ((tile_of == cols_v[...]) & (slot_lane < count)).astype(F32)
-    pick_col = jnp.concatenate([pick_col] * 3, axis=1).astype(BF16)
+    slot_lane = lax.broadcasted_iota(jnp.int32, (1, slots), 1)
+    rows_at = jnp.where(slot_lane < count, rows_v[...], -1)
+    cols_at = jnp.where(slot_lane < count, cols_v[...], -1)
+    rows_at = jnp.concatenate([rows_at, jnp.full((1, LANES - slots), -1, jnp.int32)], axis=1)
+
+    def one_hot(at, n_tiles, a=None):
+        if a is None:
+            tile = lax.broadcasted_iota(jnp.int32, (n_tiles, at.shape[1]), 0)
+        else:
+            row = lax.broadcasted_iota(jnp.int32, (n_tiles // groups, at.shape[1]), 0)
+            tile = row // quarter * per_dev + a * quarter + row % quarter
+        return (tile == at).astype(F32).astype(BF16)
+
+    n_rows, n_cols = n_col * per_dev, n_row * per_dev
+    pick_row = jnp.concatenate([one_hot(rows_at, n_rows)] * 3, axis=1)
+    pick_row_end = jnp.concatenate([one_hot(rows_at, n_rows, a) for a in range(groups) for _ in range(3)], axis=1)
+    pick_col = one_hot(jnp.concatenate([cols_at] * 3, axis=1), n_cols)
+    in_group = lax.broadcasted_iota(jnp.int32, (n_cols // groups, groups * slots), 1) // slots
+    pick_col_end = jnp.concatenate([one_hot(jnp.concatenate([cols_at] * groups, axis=1), n_cols, in_group)] * 3, axis=1)
 
     dot_lane = lax.broadcasted_iota(jnp.int32, (8, LANES), 1)
-
-    for ref in (local, backs, x_v, rh_v, msg):
+    valid = lax.broadcasted_iota(jnp.int32, (per_dev, wide), 1) < width
+
+    for ref in (local, backs, x_v, rh_v, stage):
         ref[...] = jnp.zeros_like(ref)
     rh_v[:, 0:width] = rhs[...]
 
@@ -129,7 +157,8 @@
         pltpu.make_async_copy(
             prec_hbm.at[pl.ds(k * part, part)], prec.at[pl.ds(k * part, part)], prec_sem.at[k]
         ).wait()
-        apply_blocks(prec, residual, msg.at[0], k * part, (k + 1) * part)
+        apply_blocks(prec, residual, stage, k * part, (k + 1) * part)
+    pack(stage[...], msg.at[0])
 
     pl.semaphore_wait(barrier, n_col + n_row - 2)
 
@@ -152,18 +181,23 @@
             packed = jnp.where(dot_lane == k, value, packed)
         return packed
 
+    def vector_of(got, ends, index):
+        source, tile = lax.div(index, per_dev), lax.rem(index, per_dev)
+        lanes = [got[source, pl.ds(k * per_dev + tile, 1), :] for k in range(full)]
+        return jnp.concatenate(lanes + [ends[pl.ds(index, 1), :]], axis=1)
+
     def lanes_of(packed, n):
         return [packed[0:1, k : k + 1] for k in range(n)]
 
     for j in range(ITERS):
         last = j == ITERS - 1
         got_row, got_col = got_row_of[j], got_col_of[j]
-        to_rows(lambda peer: msg.at[j], got_col.at[block(my_row)], msg_row_ssem.at[j], got_col_sem.at[j])
-        to_cols(lambda peer: msg.at[j], got_row.at[block(my_col)], msg_col_ssem.at[j], got_row_sem.at[j])
-        zh = msg[j]
+        to_rows(lambda peer: msg.at[j], got_col.at[my_row], msg_row_ssem.at[j], got_col_sem.at[j])
+        to_cols(lambda peer: msg.at[j], got_row.at[my_col], msg_col_ssem.at[j], got_row_sem.at[j])
+        zh = stage[...]
         rh = rh_v[...]
-        got_col[block(my_row), :] = zh
-        got_row[block(my_col), :] = zh
+        got_col[my_row] = msg[j]
+        got_row[my_col] = msg[j]
 
         if j == 0:
             pltpu.make_async_copy(diag_hbm, diag, diag_sem).wait()
@@ -179,52 +213,73 @@
         if j == 0:
             pltpu.make_async_copy(tile_hbm, tiles, tile_sem).wait()
         wait_bytes(got_col.at[row_blocks], got_col_sem.at[j])
+        for q in range(n_row):
+            spread(got_col[q, body:, :], col_ends, q * per_dev)
         turned_lane = lax.broadcasted_iota(jnp.int32, (width, LANES), 1)
         products = jnp.zeros((width, LANES), F32)
         for slot in range(slots):
-            index = jnp.clip(cols_s[0, slot], 0, n_row * per_dev - 1)
-            product = jnp.sum(tiles[slot] * got_col[pl.ds(index, 1), 0:width], axis=1, keepdims=True)
+            index = jnp.clip(cols_s[0, slot], 0, n_cols - 1)
+            vector = vector_of(got_col, col_ends, index)[:, 0:width]
+            product = jnp.sum(tiles[slot] * vector, axis=1, keepdims=True)
             products = jnp.where(turned_lane == slot, product, products)
-        products = jnp.where(turned_lane < count, products, 0.0)
-        products = jnp.concatenate([products, jnp.zeros((wide - width, LANES), F32)], axis=0)
-        products = lax.dot_general(
-            pick_row, jnp.concatenate(three_parts(products), axis=1),
-            (((1,), (1,)), ((), ())), preferred_element_type=F32,
+        parts = jnp.concatenate(three_parts(products), axis=1)
+        across = (((1,), (1,)), ((), ()))
+        sums = lax.dot_general(pick_row, parts[0 : full * LANES], across, preferred_element_type=F32)
+        for k in range(full):
+            out_row[j, :, k * per_dev : (k + 1) * per_dev, :] = sums[:, k * LANES : (k + 1) * LANES].reshape(n_col, per_dev, LANES)
+        ends = parts[full * LANES :]
+        gap = jnp.zeros_like(ends)
+        ends = jnp.concatenate(
+            [jnp.concatenate([ends if k == a else gap for k in range(groups)], axis=0) for a in range(groups)], axis=1
         )
-        out_row[j] = products
+        sums = lax.dot_general(pick_row_end, ends, across, preferred_element_type=F32)
+        for q in range(n_col):
+            out_row[j, q, body:, :] = sums[q * quarter : (q + 1) * quarter, :]
 
         def send_out_row():
-            to_cols(lambda peer: out_row.at[j, block(peer)], sum_row.at[j, block(my_col)], out_row_ssem.at[j], sum_row_sem.at[j])
-            sum_row[j, block(my_col), :] = out_row[j, block(my_col), :]
+            to_cols(lambda peer: out_row.at[j, peer], sum_row.at[j, my_col], out_row_ssem.at[j], sum_row_sem.at[j])
+            sum_row[j, my_col] = out_row[j, my_col]
 
         if not last:
             send_out_row()
 
         wait_bytes(got_row.at[col_blocks], got_row_sem.at[j])
-        shared = jnp.sum((out_row[j] * got_row[...]).reshape(n_col, per_dev, wide), axis=0)
-        dots[j, 2] = in_lanes(total(own + 2.0 * shared))
-        small(j, 2, last)
+
+        def send_late():
+            shared = jnp.sum(out_row[j] * got_row[...], axis=0)
+            dots[j, 2] = in_lanes(total(own) + 2.0 * total(shared))
+            small(j, 2, last)
+
         if last:
+            send_late()
             send_out_row()
         dots[j, 1] = small_sum(j, 0, True)
         small(j, 1, False)
 
+        for q in range(n_col):
+            spread(got_row[q, body:, :], row_ends, q * per_dev)
         for slot in range(slots):
-            index = jnp.clip(rows_s[0, slot], 0, n_col * per_dev - 1)
-            picked[slot : slot + 1, :] = got_row[pl.ds(index, 1), :]
+            index = jnp.clip(rows_s[0, slot], 0, n_rows - 1)
+            picked[slot : slot + 1, :] = vector_of(got_row, row_ends, index)
         turned = jnp.transpose(picked[...])
         for slot in range(slots):
             backs[slot : slot + 1, 0:width] = jnp.sum(
                 tiles[slot] * turned[0:width, slot : slot + 1], axis=0, keepdims=True
             )
-        live = lax.broadcasted_iota(jnp.int32, (slots, wide), 0) < count
-        out_col[j] = jnp.dot(
-            pick_col, jnp.concatenate(three_parts(jnp.where(live, backs[...], 0.0)), axis=0),
-            preferred_element_type=F32,
-        )
-        to_rows(lambda peer: out_col.at[j, block(peer)], sum_col.at[j, block(my_row)], out_col_ssem.at[j], sum_col_sem.at[j])
-        sum_col[j, block(my_row), :] = out_col[j, block(my_row), :]
-
+        parts = jnp.concatenate(three_parts(backs[:, 0 : full * LANES]), axis=0)
+        sums = jnp.dot(pick_col, parts, preferred_element_type=F32)
+        for k in range(full):
+            out_col[j, :, k * per_dev : (k + 1) * per_dev, :] = sums[:, k * LANES : (k + 1) * LANES].reshape(n_row, per_dev, LANES)
+        ends = backs[:, full * LANES :]
+        ends = jnp.concatenate([ends] + [pltpu.roll(ends, a * rest_lanes, 1) for a in range(1, groups)], axis=0)
+        sums = jnp.dot(pick_col_end, jnp.concatenate(three_parts(ends), axis=0), preferred_element_type=F32)
+        for q in range(n_row):
+            out_col[j, q, body:, :] = sums[q * quarter : (q + 1) * quarter, :]
+        to_rows(lambda peer: out_col.at[j, peer], sum_col.at[j, my_row], out_col_ssem.at[j], sum_col_sem.at[j])
+        sum_col[j, my_row] = out_col[j, my_row]
+
+        if not last:
+            send_late()
         dots[j, 3] = small_sum(j, 2, last)
         small(j, 3, not last)
 
@@ -257,18 +312,20 @@
             kept_s = beta * s
 
         wait_bytes(sum_col.at[j, row_blocks], sum_col_sem.at[j])
-        image = local[...]
-        for k in range(n_row):
-            image = image + sum_col[j, k * per_dev : (k + 1) * per_dev, :]
+        image = jnp.sum(sum_col[j], axis=0)
         wait_bytes(sum_row.at[j, col_blocks], sum_row_sem.at[j])
-        for k in range(n_col):
-            image = image + sum_row[j, k * per_dev : (k + 1) * per_dev, :]
+        image = image + jnp.sum(sum_row[j], axis=0)
+        for k in range(full):
+            turn[:, k * LANES : (k + 1) * LANES] = image[k * per_dev : (k + 1) * per_dev, :]
+        spread(image[body:, :], turn.at[:, pl.ds(full * LANES, LANES)], 0)
+        image = local[...] + jnp.where(valid, turn[...], 0.0)
         w = image if j == 0 else rest * image + kept_w
         s = w if j == 0 else w + kept_s
         if not last:
             rh = r - predicted * s
             rh_v[...] = rh
-            apply_blocks(prec, rh, msg.at[j + 1], 0, per_dev)
+            apply_blocks(prec, rh, stage, 0, per_dev)
+            pack(stage[...], msg.at[j + 1])
             z_v[...], w_v[...], r_v[...], s_v[...], p_v[...] = z, w, r, s, p
 
     delta_h = lanes_of(small_sum(ITERS - 1, 3, False), 1)[0]
@@ -307,10 +364,11 @@
     vmem = pl.BlockSpec(memory_space=pltpu.VMEM)
     anywhere = pl.BlockSpec(memory_space=pl.ANY)
     vector = pltpu.VMEM((per_dev, wide), F32)
-    row_area = pltpu.VMEM((ITERS, n_col * per_dev, wide), F32)
-    col_area = pltpu.VMEM((ITERS, n_row * per_dev, wide), F32)
-    got_rows = [pltpu.VMEM((n_col * per_dev, wide), F32)] * ITERS
-    got_cols = [pltpu.VMEM((n_row * per_dev, wide), F32)] * ITERS
+    length = per_dev * width // LANES
+    row_area = pltpu.VMEM((ITERS, n_col, length, LANES), F32)
+    col_area = pltpu.VMEM((ITERS, n_row, length, LANES), F32)
+    got_rows = [pltpu.VMEM((n_col, length, LANES), F32)] * ITERS
+    got_cols = [pltpu.VMEM((n_row, length, LANES), F32)] * ITERS
     each = pltpu.SemaphoreType.DMA((ITERS,))
     both = pl.pallas_call(
         functools.partial(kernel, n_row, n_col),
@@ -321,11 +379,13 @@
             pltpu.VMEM((slots, width, width), F32),
             pltpu.VMEM((per_dev, width, width), F32),
             pltpu.VMEM((per_dev, width, width), F32),
-            pltpu.VMEM((ITERS, per_dev, wide), F32),
+            pltpu.VMEM((ITERS, length, LANES), F32),
             *got_rows, *got_cols, row_area, col_area, row_area, col_area,
             pltpu.VMEM((slots, wide), F32),
             pltpu.VMEM((slots, wide), F32),
-            vector,
+            pltpu.VMEM((n_row * per_dev, LANES), F32),
+            pltpu.VMEM((n_col * per_dev, LANES), F32),
+            vector, vector, vector,
             pltpu.VMEM((ITERS, 4, 8, LANES), F32),
             pltpu.VMEM((ITERS, 4, n_row, 8, LANES), F32),
             pltpu.VMEM((ITERS, 4, n_col, 8, LANES), F32),

time: 61.1 us -> 59.8 us (0.979)
  Pallas kernels: 59.5 us -> 58.3 us
    pallas_call x1, Pallas kernels: 58.1 us -> 56.9 us  [per_device(): pl.pallas_call(functools.partial(kernel, n_row, n_col), out_shape=jax.Sha...]
where the time goes in v3:
time: 59.8 us; the launch traced here: 59.6 us
  Pallas kernels  58.3 us (97%)
  between operations  1.29 us (2%)
    pallas_call x1, Pallas kernels, per_device(): pl.pallas_call(functools.partial(kernel, n_row, n_col), out_shape=jax.Sha...  56.9 us
    pallas_call x1, Pallas kernels, per_device(): pl.pallas_call(part_kernel, out_shape=(jax.ShapeDtypeStruct((per_dev, wid...  1.42 us

profile of v3, /device:TPU:1, one launch (start us, length us, event | category | flops | bytes accessed | tf_op | source)
XLA Modules:
  0.0 59.6 jit_solution(2497463724305818870)
XLA Ops:
  1.3 56.9 %shard_map.86.both = f32[2,16,288]{2,1,0:T(8,128)} custom-call(s32[1,32]{1,0:T(1,128)} %bitcast.4, s32[1,32]{1,0:T(1,128)} %bitcast.6, s32[1,1]{1,0:T(1,128)S(6)} %copy.9.count_s, s32[1,32]{1,0:T(1,128)} %bitcast.5, s32[1,32]{1,0:T(1,128)} %bitcast.7, f32[16,288]{1,0:T(8,128)} %rhs.1, f32[16,288,288]{2,1,0:T(8,128)} %diag_hbm.1, f32[16,288,288]{2,1,0:T(8,128)} %prec_hbm.1, ...), custom_call_target="tpu_custom_call" | custom-call | tf_op jit(solution)/shard_map/pallas_call | solution.py:373
  58.2 1.4 %shard_map.87 = (f32[16,288]{1,0:T(8,128)}, f32[16,288]{1,0:T(8,128)}) custom-call(f32[2,16,288]{2,1,0:T(8,128)} %shard_map.86.both), custom_call_target="tpu_custom_call" | custom-call | tf_op jit(solution)/shard_map/pallas_call | solution.py:407

commit v4 on v3

--- a/solution.py
+++ b/solution.py
@@ -35,13 +35,14 @@
 
 def kernel(
     n_row, n_col,
-    rows_s, cols_s, count_s, rows_v, cols_v, rhs, diag_hbm, prec_hbm, tile_hbm,
+    rows_hbm, cols_hbm, count_hbm, rhs_hbm, diag_hbm, prec_hbm, tile_hbm,
     both_out,
+    rows_s, cols_s, rows_v, cols_v, count_v, rhs,
     tiles, diag, prec,
     msg, got_row0, got_row1, got_row2, got_col0, got_col1, got_col2, sum_row, sum_col, out_row, out_col,
     picked, backs, col_ends, row_ends, local, stage, turn, dots, dot_col, dot_row,
     x_v, rh_v, z_v, w_v, r_v, s_v, p_v,
-    prec_sem, diag_sem, tile_sem,
+    small_sem, prec_sem, diag_sem, tile_sem,
     msg_col_ssem, msg_row_ssem, got_row_sem, got_col_sem,
     out_row_ssem, out_col_ssem, sum_row_sem, sum_col_sem,
     dot_ssem, dot_rsem,
@@ -76,6 +77,15 @@
     for peer in row_peers:
         pl.semaphore_signal(barrier, inc=1, device_id=(peer, my_col), device_id_type=MESH)
 
+    small_copies = [
+        pltpu.make_async_copy(source, target, small_sem.at[k])
+        for k, (source, target) in enumerate((
+            (rhs_hbm, rhs), (rows_hbm, rows_v), (cols_hbm, cols_v),
+            (count_hbm, count_v), (rows_hbm, rows_s), (cols_hbm, cols_s),
+        ))
+    ]
+    for copy in small_copies:
+        copy.start()
     part = per_dev // 4
     for k in range(4):
         pltpu.make_async_copy(
@@ -124,7 +134,9 @@
     col_blocks = pl.ds(0, n_col - 1)
     row_blocks = pl.ds(0, n_row - 1)
 
-    count = count_s[0, 0]
+    for copy in small_copies:
+        copy.wait()
+    count = count_v[...]
     slot_lane = lax.broadcasted_iota(jnp.int32, (1, slots), 1)
     rows_at = jnp.where(slot_lane < count, rows_v[...], -1)
     cols_at = jnp.where(slot_lane < count, cols_v[...], -1)
@@ -253,9 +265,6 @@
         if last:
             send_late()
             send_out_row()
-        dots[j, 1] = small_sum(j, 0, True)
-        small(j, 1, False)
-
         for q in range(n_col):
             spread(got_row[q, body:, :], row_ends, q * per_dev)
         for slot in range(slots):
@@ -263,6 +272,9 @@
             picked[slot : slot + 1, :] = vector_of(got_row, row_ends, index)
         turned = jnp.transpose(picked[...])
         for slot in range(slots):
+            if slot == slots // 4:
+                dots[j, 1] = small_sum(j, 0, True)
+                small(j, 1, False)
             backs[slot : slot + 1, 0:width] = jnp.sum(
                 tiles[slot] * turned[0:width, slot : slot + 1], axis=0, keepdims=True
             )
@@ -360,9 +372,8 @@
     wide = -(-width // LANES) * LANES
     rows_here = pair_rows[0]
     cols_here = pair_cols[0]
-    smem = pl.BlockSpec(memory_space=pltpu.SMEM)
     vmem = pl.BlockSpec(memory_space=pltpu.VMEM)
-    anywhere = pl.BlockSpec(memory_space=pl.ANY)
+    hbm = pl.BlockSpec(memory_space=pltpu.HBM)
     vector = pltpu.VMEM((per_dev, wide), F32)
     length = per_dev * width // LANES
     row_area = pltpu.VMEM((ITERS, n_col, length, LANES), F32)
@@ -373,9 +384,15 @@
     both = pl.pallas_call(
         functools.partial(kernel, n_row, n_col),
         out_shape=jax.ShapeDtypeStruct((2, per_dev, width), F32),
-        in_specs=[smem, smem, smem, vmem, vmem, vmem, anywhere, anywhere, anywhere],
+        in_specs=[hbm] * 7,
         out_specs=vmem,
         scratch_shapes=[
+            pltpu.SMEM((1, slots), jnp.int32),
+            pltpu.SMEM((1, slots), jnp.int32),
+            pltpu.VMEM((1, slots), jnp.int32),
+            pltpu.VMEM((1, slots), jnp.int32),
+            pltpu.VMEM((1, 1), jnp.int32),
+            pltpu.VMEM((per_dev, width), F32),
             pltpu.VMEM((slots, width, width), F32),
             pltpu.VMEM((per_dev, width, width), F32),
             pltpu.VMEM((per_dev, width, width), F32),
@@ -390,6 +407,7 @@
             pltpu.VMEM((ITERS, 4, n_row, 8, LANES), F32),
             pltpu.VMEM((ITERS, 4, n_col, 8, LANES), F32),
             vector, vector, vector, vector, vector, vector, vector,
+            pltpu.SemaphoreType.DMA((6,)),
             pltpu.SemaphoreType.DMA((4,)),
             pltpu.SemaphoreType.DMA,
             pltpu.SemaphoreType.DMA,
@@ -401,8 +419,7 @@
             collective_id=0, has_side_effects=True, vmem_limit_bytes=56 * 2**20
         ),
     )(
-        rows_here, cols_here, tile_counts, rows_here, cols_here,
-        right_side, diag_blocks, precond, tile_values[0, 0],
+        rows_here, cols_here, tile_counts, right_side, diag_blocks, precond, tile_values[0, 0],
     )
     return pl.pallas_call(
         part_kernel,

time: 59.8 us -> 58.3 us (0.975)
  Pallas kernels: 58.3 us -> 56.8 us
    pallas_call x1, Pallas kernels: 56.9 us -> 55.4 us  [per_device(): pl.pallas_call(functools.partial(kernel, n_row, n_col), out_shape=jax.Sha...]
where the time goes in v4:
time: 58.3 us; the launch traced here: 58.1 us
  Pallas kernels  56.8 us (97%)
  between operations  1.29 us (2%)
    pallas_call x1, Pallas kernels, per_device(): pl.pallas_call(functools.partial(kernel, n_row, n_col), out_shape=jax.Sha...  55.4 us
    pallas_call x1, Pallas kernels, per_device(): pl.pallas_call(part_kernel, out_shape=(jax.ShapeDtypeStruct((per_dev, wid...  1.42 us

profile of v4, /device:TPU:1, one launch (start us, length us, event | category | flops | bytes accessed | tf_op | source)
XLA Modules:
  0.0 58.1 jit_solution(10480191834997899095)
XLA Ops:
  1.3 55.4 %shard_map.86.both = f32[2,16,288]{2,1,0:T(8,128)} custom-call(s32[1,32]{1,0:T(1,128)} %bitcast.4, s32[1,32]{1,0:T(1,128)} %bitcast.5, s32[1,1]{1,0:T(1,128)S(6)} %copy.9.count_hbm, f32[16,288]{1,0:T(8,128)} %rhs_hbm.1, f32[16,288,288]{2,1,0:T(8,128)} %diag_hbm.1, f32[16,288,288]{2,1,0:T(8,128)} %prec_hbm.1, f32[32,288,288]{2,1,0:T(8,128)} %bitcast.3), custom_call_target="tpu_custom_call" | custom-call | tf_op jit(solution)/shard_map/pallas_call | solution.py:384
  56.7 1.4 %shard_map.87 = (f32[16,288]{1,0:T(8,128)}, f32[16,288]{1,0:T(8,128)}) custom-call(f32[2,16,288]{2,1,0:T(8,128)} %shard_map.86.both), custom_call_target="tpu_custom_call" | custom-call | tf_op jit(solution)/shard_map/pallas_call | solution.py:424

commit v5 on v4

--- a/solution.py
+++ b/solution.py
@@ -62,10 +62,7 @@
     far = (2, 1, 3, 0)
     col_peers = [
         lax.rem(my_z + dz, side) * side + lax.rem(my_y + dy, side)
-        for dz, dy in sorted(
-            ((dz, dy) for dz in far for dy in far if dz or dy),
-            key=lambda d: -(min(d[0], side - d[0]) + min(d[1], side - d[1])),
-        )
+        for dz in far for dy in far if dz or dy
     ]
     row_peers = [
         lax.rem(my_x + dx, side) * 2 + lax.rem(my_core + dc, 2)
@@ -252,19 +249,17 @@
             to_cols(lambda peer: out_row.at[j, peer], sum_row.at[j, my_col], out_row_ssem.at[j], sum_row_sem.at[j])
             sum_row[j, my_col] = out_row[j, my_col]
 
-        if not last:
-            send_out_row()
+        send_out_row()
 
         wait_bytes(got_row.at[col_blocks], got_row_sem.at[j])
 
         def send_late():
             shared = jnp.sum(out_row[j] * got_row[...], axis=0)
             dots[j, 2] = in_lanes(total(own) + 2.0 * total(shared))
-            small(j, 2, last)
+            small(j, 2, False)
 
         if last:
             send_late()
-            send_out_row()
         for q in range(n_col):
             spread(got_row[q, body:, :], row_ends, q * per_dev)
         for slot in range(slots):
@@ -292,8 +287,8 @@
 
         if not last:
             send_late()
-        dots[j, 3] = small_sum(j, 2, last)
-        small(j, 3, not last)
+        dots[j, 3] = small_sum(j, 2, False)
+        small(j, 3, True)
 
         if j == 0:
             curve_h, gamma = lanes_of(small_sum(j, 1, False), 2)
@@ -340,7 +335,7 @@
             pack(stage[...], msg.at[j + 1])
             z_v[...], w_v[...], r_v[...], s_v[...], p_v[...] = z, w, r, s, p
 
-    delta_h = lanes_of(small_sum(ITERS - 1, 3, False), 1)[0]
+    delta_h = lanes_of(small_sum(ITERS - 1, 3, True), 1)[0]
     delta = rest * (rest * delta_h + twice) + theta * theta * delta
     alpha = gamma / (delta + beta * (cross + beta * curve))
     x = x_v[...] + alpha * p
@@ -354,8 +349,7 @@
         wait_bytes(sum_row.at[j, col_blocks], out_row_ssem.at[j])
         wait_bytes(sum_col.at[j, row_blocks], out_col_ssem.at[j])
         for k in range(4):
-            along_row = k == 0 or (k == 2) == (j == ITERS - 1) and k > 1
-            source, peers = (dot_row, n_col - 1) if along_row else (dot_col, n_row - 1)
+            source, peers = (dot_row, n_col - 1) if k in (0, 3) else (dot_col, n_row - 1)
             wait_bytes(source.at[j, k, pl.ds(0, peers)], dot_ssem.at[j, k])
 
 

time: 58.3 us -> 57.6 us (0.988)
  Pallas kernels: 56.8 us -> 56.1 us
    pallas_call x1, Pallas kernels: 55.4 us -> 54.7 us  [per_device(): pl.pallas_call(functools.partial(kernel, n_row, n_col), out_shape=jax.Sha...]
where the time goes in v5:
time: 57.6 us; the launch traced here: 57.4 us
  Pallas kernels  56.1 us (97%)
  between operations  1.29 us (2%)
    pallas_call x1, Pallas kernels, per_device(): pl.pallas_call(functools.partial(kernel, n_row, n_col), out_shape=jax.Sha...  54.7 us
    pallas_call x1, Pallas kernels, per_device(): pl.pallas_call(part_kernel, out_shape=(jax.ShapeDtypeStruct((per_dev, wid...  1.42 us

profile of v5, /device:TPU:1, one launch (start us, length us, event | category | flops | bytes accessed | tf_op | source)
XLA Modules:
  0.0 57.4 jit_solution(7273068686860016856)
XLA Ops:
  1.3 54.7 %shard_map.86.both = f32[2,16,288]{2,1,0:T(8,128)} custom-call(s32[1,32]{1,0:T(1,128)} %bitcast.4, s32[1,32]{1,0:T(1,128)} %bitcast.5, s32[1,1]{1,0:T(1,128)S(6)} %copy.9.count_hbm, f32[16,288]{1,0:T(8,128)} %rhs_hbm.1, f32[16,288,288]{2,1,0:T(8,128)} %diag_hbm.1, f32[16,288,288]{2,1,0:T(8,128)} %prec_hbm.1, f32[32,288,288]{2,1,0:T(8,128)} %bitcast.3), custom_call_target="tpu_custom_call" | custom-call | tf_op jit(solution)/shard_map/pallas_call | solution.py:378
  56.0 1.4 %shard_map.87 = (f32[16,288]{1,0:T(8,128)}, f32[16,288]{1,0:T(8,128)}) custom-call(f32[2,16,288]{2,1,0:T(8,128)} %shard_map.86.both), custom_call_target="tpu_custom_call" | custom-call | tf_op jit(solution)/shard_map/pallas_call | solution.py:418
